TPU v7x, 128 devices: a whole 4x4x4 slice. The times are simulated.
128 devices in a mesh: tm: 16 (over z, x), obs: 8 (over y, core).
Axes of the slice: x: 4, y: 4, z: 4, core: 2. Of those that a mesh axis runs over, the one named last changes fastest.
Arguments:
- basis: bfloat16 [2048, 128, 512], P(('tm', 'obs')), may hold values from -0.03125 to 0.03125
- obs_weight: float32 [2048, 128], P(('tm', 'obs')), may hold values from 0.2 to 5
- col_pattern: int32 [2048, 4], P(('tm', 'obs')), may hold values from 0 to 1, as said below
- tile_block: int32 [2048], P(('tm', 'obs')), may hold values from 0 to 31, as said below
- spatial_prec: float32 [512, 512], replicated, as said below
- time_coef: float32 [32], replicated, may hold values from 0.9 to 0.98
Outputs:
- sep_factor: float32 [16, 512, 512], P('tm')
Inputs may be any that keep to these rules, and one draw needn't show every extreme that they name: `col_pattern`: each tile's row holds at least one 1. `tile_block`: tile k lies in time block (k // 128) * 2 + m for some m from 0 to 1. `spatial_prec`: symmetric positive definite, smallest eigenvalue 0.5 or more.
All inputs are finite; a program needn't handle non-finite values.
Results may differ from a plain program's by a relative error of at most 0.0003.
Values sent between devices are 32-bit elements; how exact they have to be, the bound alone decides.
A program may use at most 128 MiB of HBM per device.

v0:
```python
import jax
import jax.numpy as jnp
from jax import lax
from jax.sharding import PartitionSpec as P

CT = 128
TB_DEV = 2


tiles_at_once = 4


def from_behind(block, axis, distance):
    devices = range(lax.axis_size(axis))
    route = [(i - distance, i) for i in devices if i - distance in devices]
    return lax.ppermute(block, axis, route)


def solve_lower(lower_factor, rhs):
    return lax.linalg.triangular_solve(lower_factor, rhs, left_side=True, lower=True)


def inner_dot(left_part, right_part):
    return jnp.dot(left_part.T, right_part, precision=lax.Precision.HIGHEST)


def eliminate_segment(gram_blocks, decay_rates, prior_rate, spatial_prec):
    columns = spatial_prec.shape[0]
    nblock = gram_blocks.shape[0]
    first_diag = (1.0 + decay_rates[0] * decay_rates[0]) * spatial_prec + gram_blocks[0]
    first_left = -prior_rate * spatial_prec

    def advance(position, state_tuple):
        diagonal, left_block, absorbed = state_tuple
        lower_factor = jnp.linalg.cholesky(diagonal)
        right_block = -decay_rates[position] * spatial_prec
        solved = solve_lower(lower_factor, jnp.concatenate([right_block, left_block.T], axis=1))
        solved_right = solved[:, :columns]
        solved_left = solved[:, columns:]
        rate_next = decay_rates[position + 1]
        following = (
            (1.0 + rate_next * rate_next) * spatial_prec
            + gram_blocks[position + 1]
            - inner_dot(solved_right, solved_right)
        )
        return (
            following,
            -inner_dot(solved_left, solved_right),
            absorbed + inner_dot(solved_left, solved_left),
        )

    return lax.fori_loop(
        0, nblock - 1, advance, (first_diag, first_left, jnp.zeros_like(spatial_prec))
    )


def per_device(basis, obs_weight, col_pattern, tile_block, spatial_prec, time_coef):
    own_index = lax.axis_index("tm")
    segments = lax.axis_size("tm")
    columns = spatial_prec.shape[0]
    column_mask = jnp.repeat(col_pattern.astype(jnp.float32), CT, axis=1)
    local_block = tile_block - own_index * TB_DEV

    def add_group(group, gram_blocks):
        first_tile = group * tiles_at_once
        part_basis = lax.dynamic_slice_in_dim(basis, first_tile, tiles_at_once, 0)
        part_weight = lax.dynamic_slice_in_dim(obs_weight, first_tile, tiles_at_once, 0)
        part_mask = lax.dynamic_slice_in_dim(column_mask, first_tile, tiles_at_once, 0)
        part_block = lax.dynamic_slice_in_dim(local_block, first_tile, tiles_at_once, 0)
        scaled = (jnp.sqrt(part_weight)[:, :, None] * part_basis * part_mask[:, None, :]).astype(
            jnp.bfloat16
        )
        tile_grams = jnp.einsum("kri,krj->kij", scaled, scaled, preferred_element_type=jnp.float32)
        one_hot = (part_block[:, None] == jnp.arange(TB_DEV)[None, :]).astype(jnp.float32)
        return gram_blocks + jnp.einsum(
            "kb,kij->bij", one_hot, tile_grams, precision=lax.Precision.HIGHEST
        )

    gram_local = lax.fori_loop(
        0,
        basis.shape[0] // tiles_at_once,
        add_group,
        jnp.zeros((TB_DEV, columns, columns), jnp.float32),
    )
    gram_blocks = lax.psum(gram_local, "obs")
    first_block = own_index * TB_DEV
    decay_rates = lax.dynamic_slice_in_dim(time_coef, first_block, TB_DEV)
    earlier = lax.dynamic_index_in_dim(time_coef, jnp.maximum(first_block - 1, 0), keepdims=False)
    prior_rate = jnp.where(own_index > 0, earlier, jnp.zeros_like(earlier))
    sep_diag, coupling, absorbed = eliminate_segment(
        gram_blocks, decay_rates, prior_rate, spatial_prec
    )
    from_right = from_behind(absorbed, "tm", -1)
    reduced = sep_diag - from_right
    for height in range(segments.bit_length() - 1):
        stride = 1 << height
        lower_factor = jnp.linalg.cholesky(reduced)
        solved_own = solve_lower(lower_factor, coupling.T)
        from_above = from_behind(inner_dot(solved_own, solved_own), "tm", -stride)
        coupling_above = from_behind(coupling, "tm", -stride)
        solved_next = solve_lower(lower_factor, coupling_above)
        from_below, coupling_new = from_behind(
            (inner_dot(solved_next, solved_next), -inner_dot(solved_own, solved_next)), "tm", stride
        )
        reduced = reduced - from_above - from_below
        coupling = coupling_new
    sep_factor = jnp.linalg.cholesky(reduced)
    return sep_factor[None]


def solution(mesh):
    in_specs = (
        P(("tm", "obs"), None, None),
        P(("tm", "obs"), None),
        P(("tm", "obs"), None),
        P(("tm", "obs")),
        P(),
        P(),
    )
    out_specs = P("tm", None, None)
    return jax.shard_map(
        per_device, mesh=mesh, in_specs=in_specs, out_specs=out_specs, check_vma=False
    )
```

profile of v0, /device:TPU:120, one launch (start us, length us, event | category | flops | bytes accessed | tf_op | source)
XLA Modules:
  0.0 1198.9 jit_solution(17434392606269484845)
XLA Ops:
  8.1 59.6 %while.39 = (s32[]{:T(128)}, f32[2,512,512]{2,0,1:T(2,128)S(1)}, s32[16]{0:T(128)S(1)}, f32[16,128]{1,0:T(8,128)}, bf16[16,128,512]{2,1,0:T(8,128)(2,1)}, /*inde...) while((s32[]{:T(128)}, f32[2,512,512]{2,0,1:T(2,128)S(1)}, ...), condition=%wide.region_1.0_spmd.clone, body=%wide.region_0.0_spmd.clone.sunk | while | flops 295698432 | bytes 13138141 | solution.py:79
  77.1 58.3 %all-reduce.3.cloned.1.call-done = f32[2,512,512]{1,2,0:T(8,128)} async-done(((f32[2,512,512]{1,2,0:T(8,128)}), f32[2,512,512]{1,2,0:T(8,128)}) %all-reduce.3.cloned.1.call-update) | async-done | bytes 2097168 | tf_op jit(solution)/shard_map/psum | solution.py:85
  141.0 11.7 cholesky.638
  165.2 11.7 cholesky.657
  212.2 12.1 %cholesky.695 = f32[128,128]{1,0:T(8,128)S(1)} custom-call(f32[128,128]{1,0:T(8,128)S(1)} %convolution_subtract_fusion.8), custom_call_target="Cholesky" | custom-call | tf_op jit(solution)/shard_map/while/body/eval_jaxpr/jit(cholesky)/cholesky | solution.py:35
  229.2 11.9 while.38
  241.1 39.3 %custom-call.27 = f32[4,128,128]{1,2,0:T(8,128)S(1)} custom-call(f32[4,128,128]{2,1,0:T(8,128)S(1)} %get-tuple-element.156), custom_call_target="InvertDiagBlocksLowerTriangular" | custom-call | tf_op jit(solution)/shard_map/while/body/eval_jaxpr/triangular_solve | solution.py:20
  305.4 16.0 %collective-permute-done = f32[512,512]{0,1:T(8,128)} collective-permute-done((f32[512,512]{0,1:T(8,128)S(1)}, f32[512,512]{0,1:T(8,128)}, u32[]{:S(2)}, u32[]{:S(2)}) %collective-permute-start) | collective-permute-done | bytes 1048608 | tf_op jit(solution)/shard_map/ppermute | solution.py:16
  347.9 12.1 %cholesky.729 = f32[128,128]{1,0:T(8,128)S(1)} custom-call(f32[128,128]{1,0:T(8,128)S(1)} %cholesky.1083), custom_call_target="Cholesky" | custom-call | tf_op jit(solution)/shard_map/jit(cholesky)/cholesky | solution.py:97
  394.6 11.9 cholesky.767
  418.1 39.3 %custom-call.57 = f32[4,128,128]{1,2,0:T(8,128)S(1)} custom-call(f32[4,128,128]{2,1,0:T(8,128)S(1)} %get-tuple-element.220), custom_call_target="InvertDiagBlocksLowerTriangular" | custom-call | tf_op jit(solution)/shard_map/triangular_solve/custom-call.8 | solution.py:20
  499.3 16.6 %collective-permute-done.3 = f32[512,512]{0,1:T(8,128)} collective-permute-done((f32[512,512]{0,1:T(8,128)}, f32[512,512]{0,1:T(8,128)}, u32[]{:S(2)}, u32[]{:S(2)}) %collective-permute-start.3) | collective-permute-done | bytes 1048608 | tf_op jit(solution)/shard_map/ppermute | solution.py:16
  587.4 12.1 %cholesky.839 = f32[128,128]{1,0:T(8,128)S(1)} custom-call(f32[128,128]{1,0:T(8,128)S(1)} %slice_subtract_fusion.55), custom_call_target="Cholesky" | custom-call | tf_op jit(solution)/shard_map/jit(cholesky)/cholesky | solution.py:97
  611.0 39.3 %custom-call.62 = f32[4,128,128]{1,2,0:T(8,128)S(1)} custom-call(f32[4,128,128]{2,1,0:T(8,128)S(1)} %get-tuple-element.222), custom_call_target="InvertDiagBlocksLowerTriangular" | custom-call | tf_op jit(solution)/shard_map/triangular_solve/custom-call.8 | solution.py:20
  669.1 14.4 %collective-permute-done.6 = f32[512,512]{1,0:T(8,128)S(1)} collective-permute-done((f32[512,512]{1,0:T(8,128)}, f32[512,512]{1,0:T(8,128)S(1)}, u32[]{:S(2)}, u32[]{:S(2)}) %collective-permute-start.6) | collective-permute-done | bytes 1048608 | tf_op jit(solution)/shard_map/ppermute | solution.py:16
  704.4 23.9 %collective-permute-done.7 = f32[512,512]{0,1:T(8,128)S(1)} collective-permute-done((f32[512,512]{0,1:T(8,128)}, f32[512,512]{0,1:T(8,128)S(1)}, u32[]{:S(2)}, u32[]{:S(2)}) %collective-permute-start.7) | collective-permute-done | bytes 1048608 | tf_op jit(solution)/shard_map/ppermute | solution.py:16
  799.7 11.9 cholesky.911
  823.4 39.3 %custom-call.67 = f32[4,128,128]{1,2,0:T(8,128)S(1)} custom-call(f32[4,128,128]{2,1,0:T(8,128)S(1)} %get-tuple-element.224), custom_call_target="InvertDiagBlocksLowerTriangular" | custom-call | tf_op jit(solution)/shard_map/triangular_solve/custom-call.8 | solution.py:20
  877.7 14.7 %collective-permute-done.10 = f32[512,512]{1,0:T(8,128)S(1)} collective-permute-done((f32[512,512]{1,0:T(8,128)}, f32[512,512]{1,0:T(8,128)S(1)}, u32[]{:S(2)}, u32[]{:S(2)}) %collective-permute-start.10) | collective-permute-done | bytes 1048608 | tf_op jit(solution)/shard_map/ppermute | solution.py:16
  910.6 15.4 %collective-permute-done.11 = f32[512,512]{0,1:T(8,128)S(1)} collective-permute-done((f32[512,512]{0,1:T(8,128)S(1)}, f32[512,512]{0,1:T(8,128)S(1)}, u32[]{:S(2)}, u32[]{:S(2)}) %collective-permute-start.11) | collective-permute-done | bytes 1048608 | tf_op jit(solution)/shard_map/ppermute | solution.py:16
  995.8 12.1 %cholesky.983 = f32[128,128]{1,0:T(8,128)S(1)} custom-call(f32[128,128]{1,0:T(8,128)S(1)} %slice_subtract_fusion.53), custom_call_target="Cholesky" | custom-call | tf_op jit(solution)/shard_map/jit(cholesky)/cholesky | solution.py:97
  1019.5 39.3 %custom-call.72 = f32[4,128,128]{1,2,0:T(8,128)S(1)} custom-call(f32[4,128,128]{2,1,0:T(8,128)S(1)} %get-tuple-element.226), custom_call_target="InvertDiagBlocksLowerTriangular" | custom-call | tf_op jit(solution)/shard_map/triangular_solve/custom-call.8 | solution.py:20
  1093.8 12.1 %collective-permute-done.15 = f32[512,512]{0,1:T(8,128)S(1)} collective-permute-done((f32[512,512]{0,1:T(8,128)S(1)}, f32[512,512]{0,1:T(8,128)S(1)}, u32[]{:S(2)}, u32[]{:S(2)}) %collective-permute-start.15) | collective-permute-done | bytes 1048608 | tf_op jit(solution)/shard_map/ppermute | solution.py:16
  1175.8 11.7 cholesky.1055
  (399 shorter events, 721.6 us)
Async XLA Ops:
  6.5 128.8 %all-reduce.3.cloned.1.call-start = ((), (), s32[]{:S(2)}) async-start(), calls=%async_computation | async-start | bytes 4194304 | tf_op jit(solution)/shard_map/psum | solution.py:85
  293.4 28.0 %collective-permute-start = (f32[512,512]{0,1:T(8,128)S(1)}, f32[512,512]{0,1:T(8,128)}, u32[]{:S(2)}, u32[]{:S(2)}) collective-permute-start(f32[512,512]{0,1:T(8,128)S(1)} %fusion.51), channel_id=1, source_target_pairs={{8,0},{16,8},{24,16},{32,24},{40,32},{48,40},{56,48},{64,56},{72,6... | collective-permute-start | bytes 3145736 | tf_op jit(solution)/shard_map/ppermute | solution.py:16
  298.2 23.2 %copy-start.2 = (f32[2,512,512]{1,2,0:T(8,128)S(1)}, f32[2,512,512]{1,2,0:T(8,128)}, u32[]{:S(2)}) copy-start(f32[2,512,512]{1,2,0:T(8,128)} %all-reduce.3.cloned.1.call-done) | copy-start | bytes 6291460
  302.5 173.2 %collective-permute-start.2 = (f32[512,512]{1,0:T(8,128)}, f32[512,512]{1,0:T(8,128)}, u32[]{:S(2)}, u32[]{:S(2)}) collective-permute-start(f32[512,512]{1,0:T(8,128)} %convolution_negate_fusion.3), channel_id=1, source_target_pairs={{8,0},{16,8},{24,16},{32,24},{40,32},{48,40},{56,48},{64,56},{72,6... | collective-permute-start | bytes 3145736 | tf_op jit(solution)/shard_map/ppermute | solution.py:16
  457.4 20.0 %copy-start.6 = (f32[4,128,128]{1,2,0:T(8,128)}, f32[4,128,128]{1,2,0:T(8,128)S(1)}, u32[]{:S(2)}) copy-start(f32[4,128,128]{1,2,0:T(8,128)S(1)} %custom-call.57) | copy-start | bytes 786436
  466.2 12.7 %copy-start.9 = (f32[128,512]{1,0:T(8,128)}, f32[128,512]{1,0:T(8,128)S(1)}, u32[]{:S(2)}) copy-start(f32[128,512]{1,0:T(8,128)S(1)} %fusion.336) | copy-start | bytes 786436
  469.1 30.3 %collective-permute-start.1 = (f32[512,512]{0,1:T(8,128)}, f32[512,512]{0,1:T(8,128)}, u32[]{:S(2)}, u32[]{:S(2)}) collective-permute-start(f32[512,512]{0,1:T(8,128)} %fusion.107), channel_id=1, source_target_pairs={{8,0},{16,8},{24,16},{32,24},{40,32},{48,40},{56,48},{64,56},{72,6... | collective-permute-start | bytes 3145736 | tf_op jit(solution)/shard_map/ppermute | solution.py:16
  481.3 6.3 copy-start.5
  481.3 6.3 copy-start.10
  485.7 30.3 %collective-permute-start.3 = (f32[512,512]{0,1:T(8,128)}, f32[512,512]{0,1:T(8,128)}, u32[]{:S(2)}, u32[]{:S(2)}) collective-permute-start(f32[512,512]{0,1:T(8,128)} %fusion.106), channel_id=1, source_target_pairs={{0,8},{8,16},{16,24},{24,32},{32,40},{40,48},{48,56},{56,64},{64,7... | collective-permute-start | bytes 3145736 | tf_op jit(solution)/shard_map/ppermute | solution.py:16
  490.5 159.9 %collective-permute-start.4 = (f32[512,512]{1,0:T(8,128)}, f32[512,512]{1,0:T(8,128)}, u32[]{:S(2)}, u32[]{:S(2)}) collective-permute-start(f32[512,512]{1,0:T(8,128)} %convolution_negate_fusion.2), channel_id=1, source_target_pairs={{0,8},{8,16},{16,24},{24,32},{32,40},{40,48},{48,56},{56,64},{64,7... | collective-permute-start | bytes 3145736 | tf_op jit(solution)/shard_map/ppermute | solution.py:16
  650.4 33.2 %copy-start.7 = (f32[4,128,128]{1,2,0:T(8,128)}, f32[4,128,128]{1,2,0:T(8,128)S(1)}, u32[]{:S(2)}) copy-start(f32[4,128,128]{1,2,0:T(8,128)S(1)} %custom-call.62) | copy-start | bytes 786436
  653.8 29.7 %collective-permute-start.6 = (f32[512,512]{1,0:T(8,128)}, f32[512,512]{1,0:T(8,128)S(1)}, u32[]{:S(2)}, u32[]{:S(2)}) collective-permute-start(f32[512,512]{1,0:T(8,128)} %collective-permute-done.4), channel_id=1, source_target_pairs={{16,0},{24,8},{32,16},{40,24},{48,32},{56,40},{64,48},{72,56},{80,... | collective-permute-start | bytes 3145736 | tf_op jit(solution)/shard_map/ppermute | solution.py:16
  660.9 24.7 %copy-start.11 = (f32[128,512]{1,0:T(8,128)}, f32[128,512]{1,0:T(8,128)S(1)}, u32[]{:S(2)}) copy-start(f32[128,512]{1,0:T(8,128)S(1)} %fusion.175) | copy-start | bytes 786436
  663.8 40.6 %collective-permute-start.5 = (f32[512,512]{0,1:T(8,128)}, f32[512,512]{0,1:T(8,128)}, u32[]{:S(2)}, u32[]{:S(2)}) collective-permute-start(f32[512,512]{0,1:T(8,128)} %fusion.105), channel_id=1, source_target_pairs={{16,0},{24,8},{32,16},{40,24},{48,32},{56,40},{64,48},{72,56},{80,... | collective-permute-start | bytes 3145736 | tf_op jit(solution)/shard_map/ppermute | solution.py:16
  691.2 37.2 %collective-permute-start.7 = (f32[512,512]{0,1:T(8,128)}, f32[512,512]{0,1:T(8,128)S(1)}, u32[]{:S(2)}, u32[]{:S(2)}) collective-permute-start(f32[512,512]{0,1:T(8,128)} %fusion.104), channel_id=1, source_target_pairs={{0,16},{8,24},{16,32},{24,40},{32,48},{40,56},{48,64},{56,72},{64,... | collective-permute-start | bytes 3145736 | tf_op jit(solution)/shard_map/ppermute | solution.py:16
  697.0 165.8 %collective-permute-start.8 = (f32[512,512]{1,0:T(8,128)}, f32[512,512]{1,0:T(8,128)}, u32[]{:S(2)}, u32[]{:S(2)}) collective-permute-start(f32[512,512]{1,0:T(8,128)} %convolution_negate_fusion.1), channel_id=1, source_target_pairs={{0,16},{8,24},{16,32},{24,40},{32,48},{40,56},{48,64},{56,72},{64,... | collective-permute-start | bytes 3145736 | tf_op jit(solution)/shard_map/ppermute | solution.py:16
  866.1 26.3 %collective-permute-start.10 = (f32[512,512]{1,0:T(8,128)}, f32[512,512]{1,0:T(8,128)S(1)}, u32[]{:S(2)}, u32[]{:S(2)}) collective-permute-start(f32[512,512]{1,0:T(8,128)} %collective-permute-done.8), channel_id=1, source_target_pairs={{32,0},{40,8},{48,16},{56,24},{64,32},{72,40},{80,48},{88,56},{96,... | collective-permute-start | bytes 3145736 | tf_op jit(solution)/shard_map/ppermute | solution.py:16
  875.8 34.8 %collective-permute-start.9 = (f32[512,512]{0,1:T(8,128)S(1)}, f32[512,512]{0,1:T(8,128)S(1)}, u32[]{:S(2)}, u32[]{:S(2)}) collective-permute-start(f32[512,512]{0,1:T(8,128)S(1)} %fusion.103), channel_id=1, source_target_pairs={{32,0},{40,8},{48,16},{56,24},{64,32},{72,40},{80,48},{88,56},{96,... | collective-permute-start | bytes 3145736 | tf_op jit(solution)/shard_map/ppermute | solution.py:16
  897.6 28.4 %collective-permute-start.11 = (f32[512,512]{0,1:T(8,128)S(1)}, f32[512,512]{0,1:T(8,128)S(1)}, u32[]{:S(2)}, u32[]{:S(2)}) collective-permute-start(f32[512,512]{0,1:T(8,128)S(1)} %fusion.102), channel_id=1, source_target_pairs={{0,32},{8,40},{16,48},{24,56},{32,64},{40,72},{48,80},{56,88},{64,... | collective-permute-start | bytes 3145736 | tf_op jit(solution)/shard_map/ppermute | solution.py:16
  901.7 157.1 %collective-permute-start.12 = (f32[512,512]{1,0:T(8,128)}, f32[512,512]{1,0:T(8,128)}, u32[]{:S(2)}, u32[]{:S(2)}) collective-permute-start(f32[512,512]{1,0:T(8,128)} %convolution_negate_fusion), channel_id=1, source_target_pairs={{0,32},{8,40},{16,48},{24,56},{32,64},{40,72},{48,80},{56,88},{64,... | collective-permute-start | bytes 3145736 | tf_op jit(solution)/shard_map/ppermute | solution.py:16
  1062.2 20.5 %collective-permute-start.14 = (f32[512,512]{1,0:T(8,128)}, f32[512,512]{1,0:T(8,128)S(1)}, u32[]{:S(2)}, u32[]{:S(2)}) collective-permute-start(f32[512,512]{1,0:T(8,128)} %collective-permute-done.12), channel_id=1, source_target_pairs={{64,0},{72,8},{80,16},{88,24},{96,32},{104,40},{112,48},{120,56},{... | collective-permute-start | bytes 3145736 | tf_op jit(solution)/shard_map/ppermute | solution.py:16
  1073.3 20.5 %collective-permute-start.13 = (f32[512,512]{0,1:T(8,128)S(1)}, f32[512,512]{0,1:T(8,128)S(1)}, u32[]{:S(2)}, u32[]{:S(2)}) collective-permute-start(f32[512,512]{0,1:T(8,128)S(1)} %fusion.28), channel_id=1, source_target_pairs={{64,0},{72,8},{80,16},{88,24},{96,32},{104,40},{112,48},{120,56},{... | collective-permute-start | bytes 3145736 | tf_op jit(solution)/shard_map/ppermute | solution.py:16
  1087.7 18.2 %collective-permute-start.15 = (f32[512,512]{0,1:T(8,128)S(1)}, f32[512,512]{0,1:T(8,128)S(1)}, u32[]{:S(2)}, u32[]{:S(2)}) collective-permute-start(f32[512,512]{0,1:T(8,128)S(1)} %fusion.36), channel_id=1, source_target_pairs={{0,64},{8,72},{16,80},{24,88},{32,96},{40,104},{48,112},{56,120},{... | collective-permute-start | bytes 3145736 | tf_op jit(solution)/shard_map/ppermute | solution.py:16
  (7 other events, 18.2 us)
Sparse Core Ops, SparseCore 0:
  71.1 64.2 all-reduce.2
where the time goes:
time: 1210 us; the launch traced here: 1200 us
  other arithmetic  686 us (57%)
  waiting for transfers between devices  203 us (17%)
  matrix products  171 us (14%)
  local copies, waits for them, and re-layouts  59.8 us (5%)
  starting transfers between devices  44 us (4%)
  between operations  34.5 us (3%)
    another operation x60, other arithmetic, per_device(): lower_factor = jnp.linalg.cholesky(reduced)  319 us
    another operation x12, other arithmetic, solve_lower(): lax.linalg.triangular_solve(lower_factor, rhs, left_side=True, lower=True)  198 us
    ppermute x16, waiting for transfers between devices, from_behind(): return lax.ppermute(block, axis, route)  145 us
    another operation x15, other arithmetic, per_device(): sep_factor = jnp.linalg.cholesky(reduced)  79.3 us
    another operation x14, other arithmetic, advance(): lower_factor = jnp.linalg.cholesky(diagonal)  79 us
    another operation x63, matrix products, solve_lower(): lax.linalg.triangular_solve(lower_factor, rhs, left_side=True, lower=True)  62.5 us
    psum x1, waiting for transfers between devices, per_device(): gram_blocks = lax.psum(gram_local, 'obs')  58.3 us
    ppermute x16, starting transfers between devices, from_behind(): return lax.ppermute(block, axis, route)  44 us
  transfers between devices with their start and end apart: 17, of which 13 were waited for; matrix products, arithmetic and copies ran while one was open for 50% of the time, Pallas kernels for 0%

commit v1 on v0

v1 whole, which is shorter than its diff:
```python
import jax
import jax.numpy as jnp
from jax import lax
from jax.experimental import pallas as pl
from jax.experimental.pallas import tpu as pltpu
from jax.sharding import PartitionSpec as P

CT = 128
TB_DEV = 2
BLK = 128
VMEM_LIMIT = 48 * 1024 * 1024


def from_behind(block, axis, distance):
    devices = range(lax.axis_size(axis))
    route = [(i - distance, i) for i in devices if i - distance in devices]
    return lax.ppermute(block, axis, route)


def sub_bcast(x, k):
    return jnp.broadcast_to(x[k : k + 1, :], (8, BLK))


def lane_bcast(x, c):
    return jnp.broadcast_to(x[:, c : c + 1], (8, BLK))


def inverse_factor(rows):
    lane = lax.broadcasted_iota(jnp.int32, (8, BLK), 1)
    sub = lax.broadcasted_iota(jnp.int32, (8, BLK), 0)
    rows = list(rows)
    groups = BLK // 8
    for g in range(groups):
        own = rows[g]
        cols = [lane_bcast(own, 8 * g + k) for k in range(8)]
        in_panel = (lane >= 8 * g) & (lane < 8 * g + 8)
        eye = (lane - 8 * g == sub).astype(jnp.float32)
        unit = jnp.where(in_panel, eye, own)
        full = unit
        scale = jnp.zeros((8, BLK), jnp.float32)
        for k in range(0, 8, 2):
            b0, b1 = cols[k], cols[k + 1]
            p, q, r = sub_bcast(b0, k), sub_bcast(b0, k + 1), sub_bcast(b1, k + 1)
            det = p * r - q * q
            inv = 1.0 / det
            m0 = (b0 * r - b1 * q) * inv
            m1 = (b1 * p - b0 * q) * inv
            qi = q * inv
            first, second = sub == k, sub == k + 1
            pair = first | second
            f0 = jnp.where(first, -(r * inv), jnp.where(second, qi, m0))
            f1 = jnp.where(first, qi, jnp.where(second, -(p * inv), m1))
            for j in range(k + 2, 8):
                cols[j] = (
                    jnp.where(pair, 0.0, cols[j])
                    - f0 * sub_bcast(cols[j], k)
                    - f1 * sub_bcast(cols[j], k + 1)
                )
            if g < groups - 1:
                full = (
                    jnp.where(pair, 0.0, full)
                    - f0 * sub_bcast(full, k)
                    - f1 * sub_bcast(full, k + 1)
                )
            ip = 1.0 / p
            below = sub > k + 1
            n0 = jnp.where(below, m0, jnp.where(second, q * ip, 0.0))
            n1 = jnp.where(below, m1, 0.0)
            unit = unit - n0 * sub_bcast(unit, k) - n1 * sub_bcast(unit, k + 1)
            scale = jnp.where(
                first, lax.rsqrt(p), jnp.where(second, lax.rsqrt(det * ip), scale)
            )
        rows[g] = unit * scale
        for h in range(g + 1, groups):
            below = rows[h]
            t = [lane_bcast(below, 8 * g + k) * sub_bcast(full, k) for k in range(8)]
            rows[h] = jnp.where(in_panel, 0.0, below) - (
                ((t[0] + t[1]) + (t[2] + t[3])) + ((t[4] + t[5]) + (t[6] + t[7]))
            )
    return rows


def split(x):
    hi = x.astype(jnp.bfloat16)
    return hi, (x - hi.astype(jnp.float32)).astype(jnp.bfloat16)


def as_left(x):
    hi, lo = split(x)
    return jnp.concatenate([hi, lo, hi], axis=1)


def as_right(x):
    hi, lo = split(x)
    return jnp.concatenate([hi, hi, lo], axis=1)


def dot_nt(left, right):
    return lax.dot_general(
        left, right, (((1,), (1,)), ((), ())), preferred_element_type=jnp.float32
    )


def factor_and_solve(z_ref, inv_ref, n):
    lane = lax.broadcasted_iota(jnp.int32, (8, BLK), 1)
    sub = lax.broadcasted_iota(jnp.int32, (8, BLK), 0)
    steps = n // BLK
    for k in range(steps):
        c = k * BLK
        rows = inverse_factor(
            [z_ref[c + 8 * g : c + 8 * g + 8, c : c + BLK] for g in range(BLK // 8)]
        )
        for g, row in enumerate(rows):
            inv_ref[8 * g : 8 * g + 8, :] = jnp.where(lane <= sub + 8 * g, row, 0.0)
        column = dot_nt(as_left(z_ref[c:, c : c + BLK]), as_right(inv_ref[...]))
        z_ref[c:, c : c + BLK] = column
        if k < steps - 1:
            left = as_left(column[BLK:])
            right = as_right(column[BLK : n - c])
            z_ref[c + BLK :, c + BLK :] -= dot_nt(left, right)


def scaled_tiles_gram(basis_ref, weight_ref, pattern_ref, block_ref, out_ref):
    tiles, _, columns = basis_ref.shape
    root = jnp.sqrt(weight_ref[...]).T
    lane = lax.broadcasted_iota(jnp.int32, (1, columns), 1) // CT
    out_ref[...] = jnp.zeros_like(out_ref)
    for t in range(tiles):
        mask = jnp.zeros((1, columns), jnp.float32)
        for j in range(columns // CT):
            mask = jnp.where(lane == j, pattern_ref[t, j].astype(jnp.float32), mask)
        raw = basis_ref[t].astype(jnp.float32) * mask
        x = (root[:, t : t + 1] * raw).astype(jnp.bfloat16)
        gram = lax.dot_general(
            x, x, (((0,), (0,)), ((), ())), preferred_element_type=jnp.float32
        )
        out_ref[lax.rem(block_ref[t], TB_DEV)] += gram


def segment_kernel(a_ref, v_ref, m_ref, z_ref, inv_ref):
    n = a_ref.shape[0]
    z_ref[:n] = a_ref[...]
    z_ref[n:] = v_ref[...]
    factor_and_solve(z_ref, inv_ref, n)
    solved = z_ref[n:]
    m_ref[...] = dot_nt(as_left(solved), as_right(solved))


def level_kernel(where_ref, a_ref, v_ref, out_ref, z_ref, inv_ref):
    n = a_ref.shape[0]
    part = out_ref.shape[0] // 2
    z_ref[:n] = a_ref[...]
    z_ref[n:] = v_ref[...]
    factor_and_solve(z_ref, inv_ref, n)
    start = pl.multiple_of(where_ref[0] * part, part)
    own = jnp.concatenate(
        [z_ref[pl.ds(n + start, part), :], z_ref[pl.ds(2 * n + start, part), :]], axis=0
    )
    out_ref[...] = dot_nt(as_left(own), as_right(z_ref[n:]))


def final_kernel(a_ref, l_ref, z_ref, inv_ref):
    n = a_ref.shape[0]
    z_ref[...] = a_ref[...]
    factor_and_solve(z_ref, inv_ref, n)
    row = lax.broadcasted_iota(jnp.int32, (n, n), 0)
    col = lax.broadcasted_iota(jnp.int32, (n, n), 1)
    l_ref[...] = jnp.where(col <= row, z_ref[...], 0.0)


VMEM = pl.BlockSpec(memory_space=pltpu.VMEM)
SMEM = pl.BlockSpec(memory_space=pltpu.SMEM)


def params():
    return pltpu.CompilerParams(vmem_limit_bytes=VMEM_LIMIT)


def f32(*shape):
    return jax.ShapeDtypeStruct(shape, jnp.float32)


def per_device(basis, obs_weight, col_pattern, tile_block, spatial_prec, time_coef):
    own = lax.axis_index("tm")
    segments = lax.axis_size("tm")
    where = lax.axis_index("obs")
    copies = lax.axis_size("obs")
    n = spatial_prec.shape[0]
    part = n // copies

    grams = pl.pallas_call(
        scaled_tiles_gram,
        out_shape=f32(TB_DEV, n, n),
        in_specs=[VMEM, VMEM, SMEM, SMEM],
        out_specs=VMEM,
        compiler_params=params(),
    )(basis, obs_weight, col_pattern, tile_block)
    grams = lax.psum(grams, "obs")

    first = own * TB_DEV
    last = time_coef.shape[0] - 1

    def coef(index):
        return lax.dynamic_index_in_dim(time_coef, jnp.clip(index, 0, last), keepdims=False)

    rate0, rate1 = coef(first), coef(first + 1)
    prior = jnp.where(own > 0, coef(first - 1), 0.0)
    rate_above = coef(first + 2)

    def scratch(rows):
        return [pltpu.VMEM((rows, n), jnp.float32), pltpu.VMEM((BLK, BLK), jnp.float32)]

    middle = pl.pallas_call(
        segment_kernel,
        out_shape=f32(n, n),
        in_specs=[VMEM, VMEM],
        out_specs=VMEM,
        scratch_shapes=scratch(2 * n),
        compiler_params=params(),
    )((1.0 + rate0 * rate0) * spatial_prec + grams[0], spatial_prec)

    def own_rows(x):
        return lax.dynamic_slice_in_dim(x, where * part, part, 0)

    above = from_behind(own_rows(middle), "tm", -1)
    a_rows = (
        (1.0 + rate1 * rate1) * own_rows(spatial_prec)
        + own_rows(grams[1])
        - (rate0 * rate0) * own_rows(middle)
        - (rate1 * rate1) * above
    )
    a = lax.all_gather(a_rows, "obs", axis=0, tiled=True)
    above = lax.all_gather(above, "obs", axis=0, tiled=True)
    v = jnp.concatenate([-(prior * rate0) * middle, -(rate1 * rate_above) * above], axis=0)

    for height in range(segments.bit_length() - 1):
        stride = 1 << height
        out = pl.pallas_call(
            level_kernel,
            out_shape=f32(2 * part, 2 * n),
            in_specs=[SMEM, VMEM, VMEM],
            out_specs=VMEM,
            scratch_shapes=scratch(3 * n),
            compiler_params=params(),
        )(where[None].astype(jnp.int32), a, v)
        down = from_behind(out[:part, :n], "tm", -stride)
        up = from_behind(out[part:, n:], "tm", stride)
        a_rows = a_rows - down - up
        a = lax.all_gather(a_rows, "obs", axis=0, tiled=True)
        if 2 * stride < segments:
            link = from_behind(-out[:part, n:], "tm", stride)
            link_above = from_behind(-out[part:, :n], "tm", -stride)
            v = jnp.concatenate(
                [
                    lax.all_gather(link, "obs", axis=0, tiled=True),
                    lax.all_gather(link_above, "obs", axis=0, tiled=True),
                ],
                axis=0,
            )

    factor = pl.pallas_call(
        final_kernel,
        out_shape=f32(n, n),
        in_specs=[VMEM],
        out_specs=VMEM,
        scratch_shapes=scratch(n),
        compiler_params=params(),
    )(a)
    return factor[None]


def solution(mesh):
    in_specs = (
        P(("tm", "obs"), None, None),
        P(("tm", "obs"), None),
        P(("tm", "obs"), None),
        P(("tm", "obs")),
        P(),
        P(),
    )
    out_specs = P("tm", None, None)
    return jax.shard_map(
        per_device, mesh=mesh, in_specs=in_specs, out_specs=out_specs, check_vma=False
    )
```

time: 1210 us -> 573 us (0.47)
  other arithmetic: 686 us -> 11.7 us
  matrix products: 171 us -> 0 us
  Pallas kernels: 0 us -> 136 us
  waiting for transfers between devices: 203 us -> 331 us
  local copies, waits for them, and re-layouts: 59.8 us -> 15.5 us
  between operations: 34.5 us -> 18.9 us
    another operation x101 -> x0, other arithmetic: 675 us -> none  [the longest x60 319 us: per_device(): lower_factor = jnp.linalg.cholesky(reduced)]
    all_gather x0 -> x12, waiting for transfers between devices: none -> 222 us  [the longest x5 116 us: per_device(): a = lax.all_gather(a_rows, 'obs', axis=0, tiled=True)]
    pallas_call x0 -> x7, Pallas kernels: none -> 136 us  [the longest x4 91.6 us: per_device(): pl.pallas_call(level_kernel, out_shape=f32(2 * part, 2 * n), in_specs=[SM...]
    ppermute x16 -> x15, waiting for transfers between devices: 145 us -> 46.8 us  [from_behind(): return lax.ppermute(block, axis, route)]
    dot_general x22 -> x0, matrix products: 93.4 us -> none  [the longest x4 40.4 us: add_group(): jnp.einsum('kb,kij->bij', one_hot, tile_grams, precision=lax.Precision.HI...]
    another operation x99 -> x0, matrix products: 77.3 us -> none  [the longest x63 62.5 us: solve_lower(): lax.linalg.triangular_solve(lower_factor, rhs, left_side=True, lower=True)]
    another operation x85 -> x0, local copies, waits for them, and re-layouts: 45.2 us -> none  [the longest x49 32.6 us: solve_lower(): lax.linalg.triangular_solve(lower_factor, rhs, left_side=True, lower=True)]
    ppermute x16 -> x15, starting transfers between devices: 44 us -> 50.9 us  [from_behind(): return lax.ppermute(block, axis, route)]
  transfers between devices with their start and end apart: 17 -> 28, of which waited for: 13 -> 28; matrix products, arithmetic and copies ran while one was open for 50% -> 2% of each run, Pallas kernels for 0% -> 0%
where the time goes in v1:
time: 573 us; the launch traced here: 565 us
  waiting for transfers between devices  331 us (58%)
  Pallas kernels  136 us (24%)
  starting transfers between devices  51.5 us (9%)
  between operations  18.9 us (3%)
  local copies, waits for them, and re-layouts  15.5 us (3%)
  other arithmetic  11.7 us (2%)
    all_gather x5, waiting for transfers between devices, per_device(): a = lax.all_gather(a_rows, 'obs', axis=0, tiled=True)  116 us
    pallas_call x4, Pallas kernels, per_device(): pl.pallas_call(level_kernel, out_shape=f32(2 * part, 2 * n), in_specs=[SM...  91.6 us
    all_gather x3, waiting for transfers between devices, per_device(): lax.all_gather(link_above, 'obs', axis=0, tiled=True)  74.6 us
    psum x1, waiting for transfers between devices, per_device(): grams = lax.psum(grams, 'obs')  61.8 us
    ppermute x15, starting transfers between devices, from_behind(): return lax.ppermute(block, axis, route)  50.9 us
    ppermute x15, waiting for transfers between devices, from_behind(): return lax.ppermute(block, axis, route)  46.8 us
    pallas_call x1, Pallas kernels, per_device(): pl.pallas_call(segment_kernel, out_shape=f32(n, n), in_specs=[VMEM, VMEM]...  22 us
    all_gather x1, waiting for transfers between devices, per_device(): above = lax.all_gather(above, 'obs', axis=0, tiled=True)  19.3 us
  transfers between devices with their start and end apart: 28, of which 28 were waited for; matrix products, arithmetic and copies ran while one was open for 2% of the time, Pallas kernels for 0%

profile of v1, /device:TPU:120, one launch (start us, length us, event | category | flops | bytes accessed | tf_op | source)
XLA Modules:
  0.0 564.6 jit_solution(5737273814994049548)
XLA Ops:
  17.5 61.8 %all-reduce.2.cloned.1.call-done = f32[2,512,512]{2,1,0:T(8,128)} async-done(((f32[2,512,512]{2,1,0:T(8,128)}), f32[2,512,512]{2,1,0:T(8,128)}) %all-reduce.2.cloned.1.call-update) | async-done | bytes 2097168 | tf_op jit(solution)/shard_map/psum | solution.py:198
  80.8 22.0 %shard_map.65 = f32[512,512]{1,0:T(8,128)S(1)} custom-call(f32[512,512]{1,0:T(8,128)S(1)} %fusion.a_ref, f32[512,512]{1,0:T(8,128)S(1)} %copy-done), custom_call_target="tpu_custom_call" | custom-call | tf_op jit(solution)/shard_map/pallas_call | solution.py:213
  116.7 19.3 %all-gather.15.cloned.1.call-done = f32[512,512]{1,0:T(8,128)} async-done(((f32[64,512]{1,0:T(8,128)}), f32[512,512]{1,0:T(8,128)}) %all-gather.15.cloned.1.call-update) | async-done | bytes 1048592 | tf_op jit(solution)/shard_map/all_gather | solution.py:233
  137.5 23.5 %all-gather.13.cloned.1.call-done.a_ref = f32[512,512]{1,0:T(8,128)} async-done(((f32[64,512]{1,0:T(8,128)}), f32[512,512]{1,0:T(8,128)}) %all-gather.13.cloned.1.call-update) | async-done | bytes 1048592 | tf_op jit(solution)/shard_map/all_gather | solution.py:232
  162.3 22.9 %shard_map.66 = f32[128,1024]{1,0:T(8,128)S(1)} custom-call(s32[1]{0:T(128)} %bitcast.4.where_ref, f32[512,512]{1,0:T(8,128)S(1)} %copy-done.3, f32[1024,512]{1,0:T(8,128)S(1)} %pad_maximum_fusion.v_ref), custom_call_target="tpu_custom_call" | custom-call | tf_op jit(solution)/shard_map/pallas_call | solution.py:238
  188.5 6.3 %collective-permute-done.3 = f32[64,512]{1,0:T(8,128)S(1)} collective-permute-done((f32[64,512]{1,0:T(8,128)S(1)}, f32[64,512]{1,0:T(8,128)S(1)}, u32[]{:S(2)}, u32[]{:S(2)}) %collective-permute-start.3) | collective-permute-done | bytes 131104 | tf_op jit(solution)/shard_map/ppermute | solution.py:17
  205.1 6.0 %collective-permute-start.1 = (f32[64,512]{1,0:T(8,128)S(1)}, f32[64,512]{1,0:T(8,128)S(1)}, u32[]{:S(2)}, u32[]{:S(2)}) collective-permute-start(f32[64,512]{1,0:T(8,128)S(1)} %get-tuple-element.18), channel_id=1, source_target_pairs={{8,0},{16,8},{24,16},{32,24},{40,32},{48,40},{56,48},{64,56},{72,6... | collective-permute-start | bytes 393224 | tf_op jit(solution)/shard_map/ppermute | solution.py:17
  216.7 24.8 %all-gather.21.cloned.1.call-done = f32[512,512]{1,0:T(8,128)} async-done(((f32[64,512]{1,0:T(8,128)}), f32[512,512]{1,0:T(8,128)}) %all-gather.21.cloned.1.call-update) | async-done | bytes 1048592 | tf_op jit(solution)/shard_map/all_gather | solution.py:256
  243.3 23.1 %all-gather.17.cloned.1.call-done.a_ref = f32[512,512]{1,0:T(8,128)} async-done(((f32[64,512]{1,0:T(8,128)}), f32[512,512]{1,0:T(8,128)}) %all-gather.17.cloned.1.call-update) | async-done | bytes 1048592 | tf_op jit(solution)/shard_map/all_gather | solution.py:249
  267.6 23.0 %shard_map.67 = f32[128,1024]{1,0:T(8,128)S(1)} custom-call(s32[1]{0:T(128)} %bitcast.4.where_ref, f32[512,512]{1,0:T(8,128)S(1)} %copy-done.5, f32[1024,512]{1,0:T(8,128)S(1)} %pad_maximum_fusion.1.v_ref), custom_call_target="tpu_custom_call" | custom-call | tf_op jit(solution)/shard_map/pallas_call | solution.py:238
  295.6 5.0 collective-permute-done.7
  312.4 6.3 %collective-permute-start.5 = (f32[64,512]{1,0:T(8,128)S(1)}, f32[64,512]{1,0:T(8,128)S(1)}, u32[]{:S(2)}, u32[]{:S(2)}) collective-permute-start(f32[64,512]{1,0:T(8,128)S(1)} %get-tuple-element.14), channel_id=1, source_target_pairs={{16,0},{24,8},{32,16},{40,24},{48,32},{56,40},{64,48},{72,56},{80,... | collective-permute-start | bytes 393224 | tf_op jit(solution)/shard_map/ppermute | solution.py:17
  323.8 25.0 %all-gather.27.cloned.1.call-done = f32[512,512]{1,0:T(8,128)} async-done(((f32[64,512]{1,0:T(8,128)}), f32[512,512]{1,0:T(8,128)}) %all-gather.27.cloned.1.call-update) | async-done | bytes 1048592 | tf_op jit(solution)/shard_map/all_gather | solution.py:256
  350.5 23.3 %all-gather.23.cloned.1.call-done.a_ref = f32[512,512]{1,0:T(8,128)} async-done(((f32[64,512]{1,0:T(8,128)}), f32[512,512]{1,0:T(8,128)}) %all-gather.23.cloned.1.call-update) | async-done | bytes 1048592 | tf_op jit(solution)/shard_map/all_gather | solution.py:249
  375.0 22.8 %shard_map.68 = f32[128,1024]{1,0:T(8,128)S(1)} custom-call(s32[1]{0:T(128)} %bitcast.4.where_ref, f32[512,512]{1,0:T(8,128)S(1)} %copy-done.6, f32[1024,512]{1,0:T(8,128)S(1)} %pad_maximum_fusion.2.v_ref), custom_call_target="tpu_custom_call" | custom-call | tf_op jit(solution)/shard_map/pallas_call | solution.py:238
  399.2 6.2 %collective-permute-done.11 = f32[64,512]{1,0:T(8,128)S(1)} collective-permute-done((f32[64,512]{1,0:T(8,128)S(1)}, f32[64,512]{1,0:T(8,128)S(1)}, u32[]{:S(2)}, u32[]{:S(2)}) %collective-permute-start.11) | collective-permute-done | bytes 131104 | tf_op jit(solution)/shard_map/ppermute | solution.py:17
  413.3 5.0 collective-permute-start.9
  421.6 8.0 %all-gather.31.cloned.1.call-done = f32[512,512]{1,0:T(8,128)} async-done(((f32[64,512]{1,0:T(8,128)}), f32[512,512]{1,0:T(8,128)}) %all-gather.31.cloned.1.call-update) | async-done | bytes 1048592 | tf_op jit(solution)/shard_map/all_gather | solution.py:255
  429.6 24.8 %all-gather.33.cloned.1.call-done = f32[512,512]{1,0:T(8,128)} async-done(((f32[64,512]{1,0:T(8,128)}), f32[512,512]{1,0:T(8,128)}) %all-gather.33.cloned.1.call-update) | async-done | bytes 1048592 | tf_op jit(solution)/shard_map/all_gather | solution.py:256
  456.1 23.1 %all-gather.29.cloned.1.call-done.a_ref = f32[512,512]{1,0:T(8,128)} async-done(((f32[64,512]{1,0:T(8,128)}), f32[512,512]{1,0:T(8,128)}) %all-gather.29.cloned.1.call-update) | async-done | bytes 1048592 | tf_op jit(solution)/shard_map/all_gather | solution.py:249
  480.5 22.9 %shard_map.69 = f32[128,1024]{1,0:T(8,128)S(1)} custom-call(s32[1]{0:T(128)} %bitcast.4.where_ref, f32[512,512]{1,0:T(8,128)S(1)} %copy-done.4, f32[1024,512]{1,0:T(8,128)S(1)} %pad_maximum_fusion.3.v_ref), custom_call_target="tpu_custom_call" | custom-call | tf_op jit(solution)/shard_map/pallas_call | solution.py:238
  509.7 5.6 collective-permute-done.14
  516.0 23.2 %all-gather.35.cloned.1.call-done.a_ref = f32[512,512]{1,0:T(8,128)} async-done(((f32[64,512]{1,0:T(8,128)}), f32[512,512]{1,0:T(8,128)}) %all-gather.35.cloned.1.call-update) | async-done | bytes 1048592 | tf_op jit(solution)/shard_map/all_gather | solution.py:249
  540.4 17.4 %shard_map.70 = f32[512,512]{1,0:T(8,128)} custom-call(f32[512,512]{1,0:T(8,128)S(1)} %copy-done.2), custom_call_target="tpu_custom_call" | custom-call | tf_op jit(solution)/shard_map/pallas_call | solution.py:261
  (117 shorter events, 94.3 us)
Async XLA Ops:
  6.5 72.8 %all-reduce.2.cloned.1.call-start = ((), (), s32[]{:S(2)}) async-start(), calls=%async_computation | async-start | bytes 4194304 | tf_op jit(solution)/shard_map/psum | solution.py:198
  15.0 121.0 %all-gather.15.cloned.1.call-start = ((), (), s32[]{:S(2)}) async-start(), calls=%async_computation.2 | async-start | bytes 1179648 | tf_op jit(solution)/shard_map/all_gather | solution.py:233
  102.8 8.3 %collective-permute-start = (f32[64,512]{1,0:T(8,128)S(1)}, f32[64,512]{1,0:T(8,128)S(1)}, u32[]{:S(2)}, u32[]{:S(2)}) collective-permute-start(f32[64,512]{1,0:T(8,128)S(1)} %constant_dynamic-slice_fusion), channel_id=1, source_target_pairs={{8,0},{16,8},{24,16},{32,24},{40,32},{48,40},{56,48},{64,56},{72,6... | collective-permute-start | bytes 393224 | tf_op jit(solution)/shard_map/ppermute | solution.py:17
  111.9 49.2 %all-gather.13.cloned.1.call-start = ((), (), s32[]{:S(2)}) async-start(), calls=%async_computation.1 | async-start | bytes 1179648 | tf_op jit(solution)/shard_map/all_gather | solution.py:232
  114.1 102.7 %all-gather.19.cloned.1.call-start = ((), (), s32[]{:S(2)}) async-start(), calls=%async_computation.4 | async-start | bytes 1179648 | tf_op jit(solution)/shard_map/all_gather | solution.py:255
  185.2 9.6 %collective-permute-start.3 = (f32[64,512]{1,0:T(8,128)S(1)}, f32[64,512]{1,0:T(8,128)S(1)}, u32[]{:S(2)}, u32[]{:S(2)}) collective-permute-start(f32[64,512]{1,0:T(8,128)S(1)} %get-tuple-element.15), channel_id=1, source_target_pairs={{0,8},{8,16},{16,24},{24,32},{32,40},{40,48},{48,56},{56,64},{64,7... | collective-permute-start | bytes 393224 | tf_op jit(solution)/shard_map/ppermute | solution.py:17
  195.5 46.1 %all-gather.21.cloned.1.call-start = ((), (), s32[]{:S(2)}) async-start(), calls=%async_computation.5 | async-start | bytes 1179648 | tf_op jit(solution)/shard_map/all_gather | solution.py:256
  203.1 63.3 %all-gather.17.cloned.1.call-start = ((), (), s32[]{:S(2)}) async-start(), calls=%async_computation.3 | async-start | bytes 1179648 | tf_op jit(solution)/shard_map/all_gather | solution.py:249
  203.1 9.0 %collective-permute-start.2 = (f32[64,512]{1,0:T(8,128)S(1)}, f32[64,512]{1,0:T(8,128)S(1)}, u32[]{:S(2)}, u32[]{:S(2)}) collective-permute-start(f32[64,512]{1,0:T(8,128)S(1)} %get-tuple-element.17), channel_id=1, source_target_pairs={{0,8},{8,16},{16,24},{24,32},{32,40},{40,48},{48,56},{56,64},{64,7... | collective-permute-start | bytes 393224 | tf_op jit(solution)/shard_map/ppermute | solution.py:17
  205.1 8.5 %collective-permute-start.1 = (f32[64,512]{1,0:T(8,128)S(1)}, f32[64,512]{1,0:T(8,128)S(1)}, u32[]{:S(2)}, u32[]{:S(2)}) collective-permute-start(f32[64,512]{1,0:T(8,128)S(1)} %get-tuple-element.18), channel_id=1, source_target_pairs={{8,0},{16,8},{24,16},{32,24},{40,32},{48,40},{56,48},{64,56},{72,6... | collective-permute-start | bytes 393224 | tf_op jit(solution)/shard_map/ppermute | solution.py:17
  214.3 109.5 %all-gather.25.cloned.1.call-start = ((), (), s32[]{:S(2)}) async-start(), calls=%async_computation.7 | async-start | bytes 1179648 | tf_op jit(solution)/shard_map/all_gather | solution.py:255
  290.7 9.9 %collective-permute-start.7 = (f32[64,512]{1,0:T(8,128)S(1)}, f32[64,512]{1,0:T(8,128)S(1)}, u32[]{:S(2)}, u32[]{:S(2)}) collective-permute-start(f32[64,512]{1,0:T(8,128)S(1)} %get-tuple-element.11), channel_id=1, source_target_pairs={{0,16},{8,24},{16,32},{24,40},{32,48},{40,56},{48,64},{56,72},{64,... | collective-permute-start | bytes 393224 | tf_op jit(solution)/shard_map/ppermute | solution.py:17
  301.3 47.4 %all-gather.27.cloned.1.call-start = ((), (), s32[]{:S(2)}) async-start(), calls=%async_computation.8 | async-start | bytes 1179648 | tf_op jit(solution)/shard_map/all_gather | solution.py:256
  301.4 8.4 %collective-permute-start.8 = (f32[64,512]{1,0:T(8,128)S(1)}, f32[64,512]{1,0:T(8,128)S(1)}, u32[]{:S(2)}, u32[]{:S(2)}) collective-permute-start(f32[64,512]{1,0:T(8,128)S(1)} %get-tuple-element.12), channel_id=1, source_target_pairs={{16,0},{24,8},{32,16},{40,24},{48,32},{56,40},{64,48},{72,56},{80,... | collective-permute-start | bytes 393224 | tf_op jit(solution)/shard_map/ppermute | solution.py:17
  310.4 63.3 %all-gather.23.cloned.1.call-start = ((), (), s32[]{:S(2)}) async-start(), calls=%async_computation.6 | async-start | bytes 1179648 | tf_op jit(solution)/shard_map/all_gather | solution.py:249
  310.5 9.4 %collective-permute-start.6 = (f32[64,512]{1,0:T(8,128)S(1)}, f32[64,512]{1,0:T(8,128)S(1)}, u32[]{:S(2)}, u32[]{:S(2)}) collective-permute-start(f32[64,512]{1,0:T(8,128)S(1)} %get-tuple-element.13), channel_id=1, source_target_pairs={{0,16},{8,24},{16,32},{24,40},{32,48},{40,56},{48,64},{56,72},{64,... | collective-permute-start | bytes 393224 | tf_op jit(solution)/shard_map/ppermute | solution.py:17
  312.4 8.8 %collective-permute-start.5 = (f32[64,512]{1,0:T(8,128)S(1)}, f32[64,512]{1,0:T(8,128)S(1)}, u32[]{:S(2)}, u32[]{:S(2)}) collective-permute-start(f32[64,512]{1,0:T(8,128)S(1)} %get-tuple-element.14), channel_id=1, source_target_pairs={{16,0},{24,8},{32,16},{40,24},{48,32},{56,40},{64,48},{72,56},{80,... | collective-permute-start | bytes 393224 | tf_op jit(solution)/shard_map/ppermute | solution.py:17
  322.0 107.6 %all-gather.31.cloned.1.call-start = ((), (), s32[]{:S(2)}) async-start(), calls=%async_computation.10 | async-start | bytes 1179648 | tf_op jit(solution)/shard_map/all_gather | solution.py:255
  397.9 7.5 %collective-permute-start.11 = (f32[64,512]{1,0:T(8,128)S(1)}, f32[64,512]{1,0:T(8,128)S(1)}, u32[]{:S(2)}, u32[]{:S(2)}) collective-permute-start(f32[64,512]{1,0:T(8,128)S(1)} %get-tuple-element.7), channel_id=1, source_target_pairs={{0,32},{8,40},{16,48},{24,56},{32,64},{40,72},{48,80},{56,88},{64,... | collective-permute-start | bytes 393224 | tf_op jit(solution)/shard_map/ppermute | solution.py:17
  406.1 48.4 %all-gather.33.cloned.1.call-start = ((), (), s32[]{:S(2)}) async-start(), calls=%async_computation.11 | async-start | bytes 1179648 | tf_op jit(solution)/shard_map/all_gather | solution.py:256
  412.0 67.3 %all-gather.29.cloned.1.call-start = ((), (), s32[]{:S(2)}) async-start(), calls=%async_computation.9 | async-start | bytes 1179648 | tf_op jit(solution)/shard_map/all_gather | solution.py:249
  413.3 7.5 %collective-permute-start.9 = (f32[64,512]{1,0:T(8,128)S(1)}, f32[64,512]{1,0:T(8,128)S(1)}, u32[]{:S(2)}, u32[]{:S(2)}) collective-permute-start(f32[64,512]{1,0:T(8,128)S(1)} %get-tuple-element.10), channel_id=1, source_target_pairs={{32,0},{40,8},{48,16},{56,24},{64,32},{72,40},{80,48},{88,56},{96,... | collective-permute-start | bytes 393224 | tf_op jit(solution)/shard_map/ppermute | solution.py:17
  421.5 117.7 %all-gather.35.cloned.1.call-start = ((), (), s32[]{:S(2)}) async-start(), calls=%async_computation.12 | async-start | bytes 1179648 | tf_op jit(solution)/shard_map/all_gather | solution.py:249
  506.6 8.8 %collective-permute-start.14 = (f32[64,512]{1,0:T(8,128)S(1)}, f32[64,512]{1,0:T(8,128)S(1)}, u32[]{:S(2)}, u32[]{:S(2)}) collective-permute-start(f32[64,512]{1,0:T(8,128)S(1)} %get-tuple-element.6), channel_id=1, source_target_pairs={{0,64},{8,72},{16,80},{24,88},{32,96},{40,104},{48,112},{56,120},{... | collective-permute-start | bytes 393224 | tf_op jit(solution)/shard_map/ppermute | solution.py:17
  (27 other events, 324.0 us)
Sparse Core Ops, SparseCore 0:
  15.1 64.1 all-reduce.1
  112.0 24.0 all-gather.14
  137.8 23.2 all-gather.12
  195.6 21.1 all-gather.18
  218.3 23.2 all-gather.20
  243.1 23.2 all-gather.16
  301.5 22.3 all-gather.24
  325.5 23.2 all-gather.26
  350.5 23.2 all-gather.22
  406.2 23.3 all-gather.30
  431.3 23.0 all-gather.32
  456.0 23.2 all-gather.28
  516.2 23.0 all-gather.34
